TPU v7x, 32 devices: a whole 2x2x4 slice. The times are simulated.
32 devices in a mesh: req: 16 (over z, y, x), tp: 2 (over core).
Axes of the slice: x: 2, y: 2, z: 4, core: 2. Of those that a mesh axis runs over, the one named last changes fastest.
Arguments:
- hidden_in: bfloat16 [512, 24, 3072], P(('req', 'tp')), may hold values from -6 to 6
- norm_gain: float32 [3072], replicated, may hold values from 0.1 to 1.9
- w_q: bfloat16 [3072, 3072], P(None, 'tp'), may hold values from -0.108253175 to 0.108253175
- w_k: bfloat16 [3072, 3072], P(None, 'tp'), may hold values from -3.35584844 to 3.35584844
- w_v: bfloat16 [3072, 3072], P(None, 'tp'), may hold values from -0.109375 to 0.109375
- w_o: bfloat16 [3072, 3072], P('tp'), may hold values from -0.109375 to 0.109375
- lengths: int32 [16, 32], P('req'), may hold values from 1 to 24, 576 in all within a row
- dest: int32 [16, 32, 1], P('req'), may hold values from 0 to 15; in each aligned block of 32 rows (0 to 31, 32 to 63, ..., all dimensions but the last counted through in order) at most 2 rows name the same one
Outputs:
- hidden_out: bfloat16 [512, 24, 3072], P(('req', 'tp'))
- cache: bfloat16 [512, 24, 2, 3072], P('req', None, None, 'tp')
Inputs may be any that keep to these rules, and one draw needn't show every extreme that they name: Each replica's lengths sum to 576 and the longest is 24. `dest`: no replica names one destination for more than 2 of its requests, and some replica names one exactly 2 times.
All inputs are finite; a program needn't handle non-finite values.
Results may differ from a plain program's by a relative error of at most 0.015.
Values may be sent and summed in bfloat16 or wider, within the bound.
A program may use at most 128 MiB of HBM per device.

v0:
```python
import functools

import jax
import jax.numpy as jnp
from jax import lax
from jax.experimental import pallas as pl
from jax.experimental.pallas import tpu as pltpu
from jax.sharding import PartitionSpec as P

HD = 96
CAP = 2
EPS = 1e-05
GROUP = 384
PAIR = 2 * HD
BLOCK = 96
VMEM = 56 * 1024 * 1024


def rope_tables(slot):
    pos = jnp.arange(slot, dtype=jnp.float32)
    inv = 10000.0 ** (-(jnp.arange(HD // 2, dtype=jnp.float32) * 2.0) / HD)
    angle = pos[:, None] * inv[None, :]
    cosine, sine = jnp.cos(angle), jnp.sin(angle)
    zero = jnp.zeros_like(sine)
    heads = GROUP // HD
    cosine = jnp.tile(jnp.concatenate([cosine, cosine], -1), (1, heads))
    low = jnp.tile(jnp.concatenate([-sine, zero], -1), (1, heads))
    high = jnp.tile(jnp.concatenate([zero, sine], -1), (1, heads))
    return cosine, low, high


def rotate(x, cosine, low, high):
    rows, width = x.shape
    slot = cosine.shape[0]
    half = HD // 2
    up = pltpu.roll(x, width - half, 1)
    down = pltpu.roll(x, half, 1)
    shape = (rows // slot, slot, width)
    y = (
        x.reshape(shape) * cosine[None]
        + up.reshape(shape) * low[None]
        + down.reshape(shape) * high[None]
    )
    return y.reshape(rows, width)


def normalise(x, gain):
    xf = x.astype(jnp.float32)
    mean_sq = jnp.mean(xf * xf, -1, keepdims=True)
    return xf * lax.rsqrt(mean_sq + EPS) * gain


def attention(q, k, v, bias):
    lane = lax.broadcasted_iota(jnp.int32, (BLOCK, GROUP), 1)
    outs = []
    for pair in range(GROUP // PAIR):
        lo = 128 * pair
        cols = slice(lo, lo + 256)
        place = lane[:, cols]
        first = PAIR * pair
        own = [
            (place >= first + HD * j) & (place < first + HD * (j + 1)) for j in range(2)
        ]
        qp, kp, vp = q[:, cols], k[:, cols], v[:, cols]
        zero = jnp.zeros_like(qp)
        stacked = jnp.concatenate([jnp.where(m, qp, zero) for m in own], 0)
        s = lax.dot_general(
            stacked, kp, (((1,), (1,)), ((), ())), preferred_element_type=jnp.float32
        )
        s = s * (1.0 / HD**0.5) + jnp.concatenate([bias, bias], 0)
        e = jnp.exp(s - jnp.max(s, -1, keepdims=True))
        p = (e / jnp.sum(e, -1, keepdims=True)).astype(jnp.bfloat16)
        o = jnp.dot(p, vp, preferred_element_type=jnp.float32)
        outs.append(
            jnp.where(own[0], o[:BLOCK], jnp.where(own[1], o[BLOCK:], 0.0))
        )
    left, right = outs
    return jnp.concatenate(
        [left[:, :128], left[:, 128:] + right[:, :128], right[:, 128:]], 1
    )


def attend_kernel(
    chunk, x_ref, gain_ref, wq_ref, wk_ref, wv_ref, cos_ref, low_ref, high_ref, bias_ref,
    out_ref, normed_ref,
):
    rows = normed_ref.shape[0]

    @pl.when(pl.program_id(0) == 0)
    def _():
        def body(i, carry):
            at = pl.ds(pl.multiple_of(i * BLOCK, BLOCK), BLOCK)
            normed_ref[at, :] = normalise(x_ref[at, :], gain_ref[...]).astype(jnp.bfloat16)
            return carry

        lax.fori_loop(0, rows // BLOCK, body, 0)

    cosine, low, high = cos_ref[...], low_ref[...], high_ref[...]

    def body(i, carry):
        base = pl.multiple_of(i * chunk, chunk)
        n = normed_ref[pl.ds(base, chunk), :]
        dot = functools.partial(jnp.dot, preferred_element_type=jnp.float32)
        q = rotate(dot(n, wq_ref[...]), cosine, low, high).astype(jnp.bfloat16)
        k = rotate(dot(n, wk_ref[...]), cosine, low, high).astype(jnp.bfloat16)
        v = dot(n, wv_ref[...]).astype(jnp.bfloat16)
        for b in range(chunk // BLOCK):
            at = slice(b * BLOCK, (b + 1) * BLOCK)
            o = attention(q[at], k[at], v[at], bias_ref[i * (chunk // BLOCK) + b])
            out_ref[pl.ds(pl.multiple_of(base + b * BLOCK, BLOCK), BLOCK), :] = o.astype(
                jnp.bfloat16
            )
        return carry

    lax.fori_loop(0, rows // chunk, body, 0)


def attend(x, gain, w_q, w_k, w_v, tables, bias):
    rows, width = x.shape
    per_dev = w_q.shape[1]
    slot = tables[0].shape[0]
    whole = lambda shape: pl.BlockSpec(shape, lambda g: (0,) * len(shape))
    weight = pl.BlockSpec((width, GROUP), lambda g: (0, g))
    return pl.pallas_call(
        functools.partial(attend_kernel, 384),
        grid=(per_dev // GROUP,),
        in_specs=[
            whole((rows, width)), whole((1, width)), weight, weight, weight,
            whole((slot, GROUP)), whole((slot, GROUP)), whole((slot, GROUP)),
            whole(bias.shape),
        ],
        out_specs=pl.BlockSpec((rows, GROUP), lambda g: (0, g)),
        out_shape=jax.ShapeDtypeStruct((rows, per_dev), jnp.bfloat16),
        scratch_shapes=[pltpu.VMEM((rows, width), jnp.bfloat16)],
        compiler_params=pltpu.CompilerParams(vmem_limit_bytes=VMEM),
        cost_estimate=pl.CostEstimate(
            flops=2 * rows * width * per_dev * 3,
            bytes_accessed=2 * (rows * width + 3 * width * per_dev + rows * per_dev),
            transcendentals=0,
        ),
        name="attend",
    )(x, gain, w_q, w_k, w_v, *tables, bias)


def cache_kernel(x_ref, gain_ref, wk_ref, wv_ref, cos_ref, low_ref, high_ref, k_ref, v_ref, normed_ref):
    cap, sources, slot, width = x_ref.shape

    @pl.when(pl.program_id(0) == 0)
    def _():
        def body(i, carry):
            both = [normalise(x_ref[c, i], gain_ref[...]) for c in range(cap)]
            span = cap * slot
            at = pl.ds(pl.multiple_of(i * span, span), span)
            normed_ref[at, :] = jnp.concatenate(both, 0).astype(jnp.bfloat16)
            return carry

        lax.fori_loop(0, sources, body, 0)

    cosine, low, high = cos_ref[...], low_ref[...], high_ref[...]
    rows = normed_ref.shape[0]
    chunk = 384

    def body(i, carry):
        at = pl.ds(pl.multiple_of(i * chunk, chunk), chunk)
        n = normed_ref[at, :]
        dot = functools.partial(jnp.dot, preferred_element_type=jnp.float32)
        k_ref[at, :] = rotate(dot(n, wk_ref[...]), cosine, low, high).astype(jnp.bfloat16)
        v_ref[at, :] = dot(n, wv_ref[...]).astype(jnp.bfloat16)
        return carry

    lax.fori_loop(0, rows // chunk, body, 0)


def cache_rows(x, gain, w_k, w_v, tables):
    cap, sources, slot, width = x.shape
    rows = cap * sources * slot
    per_dev = w_k.shape[1]
    whole = lambda shape: pl.BlockSpec(shape, lambda g: (0,) * len(shape))
    single = lambda shape: pl.BlockSpec(
        shape, lambda g: (0,) * len(shape), pipeline_mode=pl.Buffered(1)
    )
    weight = pl.BlockSpec((width, GROUP), lambda g: (0, g))
    out = pl.BlockSpec((rows, GROUP), lambda g: (0, g))
    return pl.pallas_call(
        cache_kernel,
        grid=(per_dev // GROUP,),
        in_specs=[
            single(x.shape), whole((1, width)), weight, weight,
            whole((slot, GROUP)), whole((slot, GROUP)), whole((slot, GROUP)),
        ],
        out_specs=[out, out],
        out_shape=[jax.ShapeDtypeStruct((rows, per_dev), jnp.bfloat16)] * 2,
        scratch_shapes=[pltpu.VMEM((rows, width), jnp.bfloat16)],
        compiler_params=pltpu.CompilerParams(vmem_limit_bytes=VMEM),
        cost_estimate=pl.CostEstimate(
            flops=2 * rows * width * per_dev * 2,
            bytes_accessed=2 * (rows * width + 2 * width * per_dev + 2 * rows * per_dev),
            transcendentals=0,
        ),
        name="cache_rows",
    )(x, gain, w_k, w_v, *tables)


def pick_kernel(source_ref, lens_ref, x_ref, out_ref):
    slots, slot, width = out_ref.shape

    def body(i, carry):
        place = lax.broadcasted_iota(jnp.int32, (slot, width), 0)
        rows = x_ref[source_ref[i]].astype(jnp.float32)
        out_ref[i] = jnp.where(place < lens_ref[i], rows, 0.0).astype(jnp.bfloat16)
        return carry

    lax.fori_loop(0, slots, body, 0)


def pick(x, source, lens):
    _, slot, width = x.shape
    slots = source.shape[0]
    return pl.pallas_call(
        pick_kernel,
        in_specs=[
            pl.BlockSpec(memory_space=pltpu.SMEM),
            pl.BlockSpec(memory_space=pltpu.SMEM),
            pl.BlockSpec(memory_space=pltpu.VMEM),
        ],
        out_specs=pl.BlockSpec(memory_space=pltpu.VMEM),
        out_shape=jax.ShapeDtypeStruct((slots, slot, width), jnp.bfloat16),
        compiler_params=pltpu.CompilerParams(vmem_limit_bytes=VMEM),
        name="pick",
    )(source, lens, x)


def exchange(blocks, axis):
    return lax.all_to_all(blocks, axis, split_axis=0, concat_axis=0, tiled=True)


def on_device(hidden_in, norm_gain, w_q, w_k, w_v, w_o, lengths, dest):
    req_dev, slot, width = hidden_in.shape
    group = lax.axis_size("tp")
    me = lax.axis_index("tp")
    req_rep = req_dev * group
    n_req = lax.axis_size("req")
    tables = rope_tables(slot)
    gain = norm_gain[None, :]
    lens = lengths[0]

    x_all = lax.all_gather(hidden_in, "tp", axis=0, tiled=True)

    target = dest[0, :, 0]
    same = target[:, None] == target[None, :]
    earlier = jnp.arange(req_rep)[None, :] < jnp.arange(req_rep)[:, None]
    rank = jnp.sum((same & earlier).astype(jnp.int32), -1)
    wanted = jnp.arange(n_req, dtype=jnp.int32)[:, None]
    my_rank = me % CAP
    fills = (target[None, :] == wanted) & (rank[None, :] == my_rank)
    source = jnp.sum(jnp.where(fills, jnp.arange(req_rep, dtype=jnp.int32)[None, :], 0), -1)
    slot_len = jnp.sum(jnp.where(fills, lens[None, :], 0), -1)

    shares = group // CAP
    part = width // shares
    outbound = pick(x_all, source, slot_len)
    if shares > 1:
        outbound = lax.dynamic_slice_in_dim(outbound, (me // CAP) * part, part, 2)
    inbound = exchange(outbound, "req")

    live = jnp.arange(slot, dtype=jnp.int32)[None, :] < lens[:, None]
    per_block = BLOCK // slot
    token = jnp.arange(BLOCK)
    inside = (token[None, :] // slot == token[:, None] // slot) & (
        token[None, :] <= token[:, None]
    )
    bias = jnp.where(
        inside[None] & live.reshape(req_rep // per_block, 1, BLOCK), 0.0, -1e30
    ).astype(jnp.float32)
    attn = attend(x_all.reshape(req_rep * slot, width), gain, w_q, w_k, w_v, tables, bias)
    partial = jnp.dot(attn, w_o, preferred_element_type=jnp.float32).astype(jnp.bfloat16)
    partial = partial.reshape(group, req_dev, slot, width)
    mine = lax.dynamic_index_in_dim(partial, me, 0, keepdims=False).astype(jnp.float32)
    total = mine
    for step in range(1, group):
        sent = lax.dynamic_index_in_dim(partial, (me + step) % group, 0, keepdims=False)
        came = lax.ppermute(sent, "tp", [(i, (i + step) % group) for i in range(group)])
        total = total + came.astype(jnp.float32)
    hidden_out = (total + hidden_in.astype(jnp.float32)).astype(jnp.bfloat16)

    kept = lax.all_gather(inbound, "tp", axis=0, tiled=False)
    if shares > 1:
        kept = kept.reshape(shares, CAP, n_req, slot, part)
        kept = kept.transpose(1, 2, 3, 0, 4).reshape(CAP, n_req, slot, width)
    keys, values = cache_rows(kept, gain, w_k, w_v, tables)
    cache = jnp.stack([keys, values], 1).reshape(n_req * CAP, slot, 2, w_k.shape[1])
    return hidden_out, cache


def solution(mesh):
    placed = (
        P(("req", "tp"), None, None),
        P(),
        P(None, "tp"),
        P(None, "tp"),
        P(None, "tp"),
        P("tp", None),
        P("req", None),
        P("req", None, None),
    )
    return jax.shard_map(
        on_device,
        mesh=mesh,
        in_specs=placed,
        out_specs=(P(("req", "tp"), None, None), P("req", None, None, "tp")),
        check_vma=False,
    )
```

profile of v0, /device:TPU:15, one launch (start us, length us, event | category | flops | bytes accessed | tf_op | source)
XLA Modules:
  0.0 181.4 jit_solution(14845874970336139429)
XLA Ops:
  7.2 0.7 all-gather.4.cloned.1.call-update
  7.9 0.9 convert_reduce_fusion
  8.8 1.3 select_reduce_fusion
  10.1 15.7 %all-gather.4.cloned.1.call-done.x_ref = bf16[32,24,3072]{2,1,0:T(8,128)(2,1)} async-done(((bf16[16,24,3072]{2,1,0:T(8,128)(2,1)}), bf16[32,24,3072]{2,1,0:T(8,128)(2,1)}) %all-gather.4.cloned.1.call-update) | async-done | bytes 4718608 | tf_op jit(solution)/shard_map/all_gather | solution.py:247
  25.8 4.3 %pick.1 = bf16[16,24,3072]{2,1,0:T(8,128)(2,1)} custom-call(s32[16]{0:T(128)} %get-tuple-element.7.source_ref, s32[16]{0:T(128)} %get-tuple-element.6.lens_ref, bf16[32,24,3072]{2,1,0:T(8,128)(2,1)} %all-gather.4.cloned.1.call-done.x_ref), custom_call_target="tpu_custom_call" | custom-call | tf_op jit(solution)/shard_map/pick/pallas_call | solution.py:219
  30.1 6.4 %all-to-all-start = ((bf16[16,24,3072]{2,1,0:T(8,128)(2,1)}), bf16[16,24,3072]{2,1,0:T(8,128)(2,1)S(1)}, u32[]{:S(2)}, u32[]{:S(2)}) async-start(bf16[16,24,3072]{2,1,0:T(8,128)(2,1)} %pick.1), calls=%async_computation | async-start | bytes 4718592 | tf_op jit(solution)/shard_map/all_to_all | solution.py:234
  36.7 0.7 tile.13.cos_ref
  37.4 0.7 tile.30.low_ref
  38.2 0.7 tile.32.high_ref
  39.4 0.7 reduce.3
  40.5 0.8 and_select_fusion.bias_ref
  41.4 46.6 %attend.1 = bf16[768,1536]{1,0:T(8,128)(2,1)} custom-call(bf16[768,3072]{1,0:T(8,128)(2,1)} %bitcast.15, f32[1,3072]{1,0:T(1,128)} %bitcast.24, bf16[3072,1536]{1,0:T(8,128)(2,1)} %wq_ref.1, bf16[3072,1536]{1,0:T(8,128)(2,1)} %wk_ref.3, bf16[3072,1536]{1,0:T(8,128)(2,1)} %wv_ref.3, f32[24,384]{1,0:T(8,128)} %tile.13.cos_ref, f32[24,384]{1,0:T(8,128)} %tile.30.low_ref, ...), custom_call_target="tpu_custom_call" | custom-call | flops 21743271936 | bytes 35389440 | tf_op jit(solution)/shard_map/attend/pallas_call | solution.py:124
  88.0 2.2 %all-to-all-done = bf16[16,24,3072]{2,1,0:T(8,128)(2,1)S(1)} async-done(((bf16[16,24,3072]{2,1,0:T(8,128)(2,1)}), bf16[16,24,3072]{2,1,0:T(8,128)(2,1)S(1)}, u32[]{:S(2)}, u32[]{:S(2)}) %all-to-all-start) | async-done | bytes 2359328 | tf_op jit(solution)/shard_map/all_to_all | solution.py:234
  90.2 1.4 copy-done
  91.6 10.8 %convolution_convert_fusion = bf16[768,3072]{1,0:T(8,128)(2,1)S(1)} fusion(bf16[768,1536]{1,0:T(8,128)(2,1)} %attend.1, bf16[1536,3072]{1,0:T(8,128)(2,1)} %param.13), kind=kOutput, calls=%fused_computation | convolution fusion | flops 7250116608 | bytes 16515072 | tf_op jit(solution)/shard_map/dot_general | solution.py:276
  102.4 2.5 %copy-done.2 = bf16[768,3072]{1,0:T(8,128)(2,1)} copy-done((bf16[768,3072]{1,0:T(8,128)(2,1)}, bf16[768,3072]{1,0:T(8,128)(2,1)S(1)}, u32[]{:S(2)}) %copy-start.2) | copy-done | bytes 4718616
  104.9 1.6 dynamic-slice_bitcast_fusion
  106.4 1.3 collective-permute-start
  107.7 4.5 %collective-permute-done = bf16[16,24,3072]{2,1,0:T(8,128)(2,1)} collective-permute-done((bf16[16,24,3072]{2,1,0:T(8,128)(2,1)}, bf16[16,24,3072]{2,1,0:T(8,128)(2,1)}, u32[]{:S(2)}, u32[]{:S(2)}) %collective-permute-start) | collective-permute-done | bytes 2359328 | tf_op jit(solution)/shard_map/ppermute | solution.py:282
  112.2 5.0 %fusion.1 = bf16[16,24,3072]{2,1,0:T(8,128)(2,1)} fusion(bf16[16,24,3072]{2,1,0:T(8,128)(2,1)S(1)} %copy-done.1, bf16[16,24,3072]{2,1,0:T(8,128)(2,1)} %collective-permute-done, bf16[2,16,24,3072]{3,2,1,0:T(8,128)(2,1)} %bitcast.17, s32[]{:T(128)S(6)} %select_n.49), kind=kLoop, calls=%fused_computation.4 | loop fusion | flops 7077888 | bytes 9437188 | tf_op jit(solution)/shard_map/convert_element_type | solution.py:284
  117.2 28.6 %cache_rows.1 = (bf16[768,1536]{1,0:T(8,128)(2,1)}, bf16[768,1536]{1,0:T(8,128)(2,1)}) custom-call(bf16[2,16,24,3072]{3,2,1,0:T(8,128)(2,1)} %bitcast.23, f32[1,3072]{1,0:T(1,128)} %bitcast.25, bf16[3072,1536]{1,0:T(8,128)(2,1)} %wk_ref.3, bf16[3072,1536]{1,0:T(8,128)(2,1)} %wv_ref.3, f32[24,384]{1,0:T(8,128)} %tile.13.cos_ref, f32[24,384]{1,0:T(8,128)} %tile.30.low_ref, ...), custom_call_target="tpu_custom_call" | custom-call | flops 14495514624 | bytes 28311552 | tf_op jit(solution)/shard_map/cache_rows/pallas_call | solution.py:184
  145.8 6.9 %copy.17 = bf16[32,24,1,1536]{3,2,1,0:T(2,128)(2,1)S(1)} copy(bf16[32,24,1,1536]{3,1,0,2:T(8,128)(2,1)} %bitcast.19) | data formatting | bytes 4718592 | tf_op jit(solution)/shard_map/stack | solution.py:291
  152.7 9.0 %copy.16 = bf16[32,24,1,1536]{3,2,1,0:T(2,128)(2,1)} copy(bf16[32,24,1,1536]{3,1,0,2:T(8,128)(2,1)} %bitcast.18) | data formatting | bytes 4718592 | tf_op jit(solution)/shard_map/stack | solution.py:291
  161.7 12.8 %pad_maximum_fusion = bf16[32,24,2,1536]{3,2,1,0:T(2,128)(2,1)} fusion(bf16[32,24,1,1536]{3,2,1,0:T(2,128)(2,1)S(1)} %copy.17, bf16[32,24,1,1536]{3,2,1,0:T(2,128)(2,1)} %copy.16), kind=kLoop, calls=%fused_computation.1 | loop fusion | flops 9437184 | bytes 9437184 | tf_op jit(solution)/shard_map/stack | solution.py:291
  (28 shorter events, 1.3 us)
Async XLA Ops:
  7.2 18.7 %all-gather.4.cloned.1.call-start = ((), (), s32[]{:S(2)}) async-start(), calls=%async_computation.1 | async-start | bytes 7077888 | tf_op jit(solution)/shard_map/all_gather | solution.py:247
  25.8 13.6 %copy-start.3 = (s32[1,32]{1,0:T(1,128)S(1)}, s32[1,32]{1,0:T(1,128)}, u32[]{:S(2)}) copy-start(s32[1,32]{1,0:T(1,128)} %param.14) | copy-start | bytes 388
  30.1 60.1 %all-to-all-start = ((bf16[16,24,3072]{2,1,0:T(8,128)(2,1)}), bf16[16,24,3072]{2,1,0:T(8,128)(2,1)S(1)}, u32[]{:S(2)}, u32[]{:S(2)}) async-start(bf16[16,24,3072]{2,1,0:T(8,128)(2,1)} %pick.1), calls=%async_computation | async-start | bytes 4718592 | tf_op jit(solution)/shard_map/all_to_all | solution.py:234
  36.5 80.7 %all-gather.6.cloned.1.call-start = ((), (), s32[]{:S(2)}) async-start(), calls=%async_computation.2 | async-start | bytes 7077888 | tf_op jit(solution)/shard_map/all_gather | solution.py:286
  90.2 1.4 copy-start
  102.4 2.5 %copy-start.2 = (bf16[768,3072]{1,0:T(8,128)(2,1)}, bf16[768,3072]{1,0:T(8,128)(2,1)S(1)}, u32[]{:S(2)}) copy-start(bf16[768,3072]{1,0:T(8,128)(2,1)S(1)} %convolution_convert_fusion) | copy-start | bytes 14155780
  102.4 9.8 %copy-start.1 = (bf16[16,24,3072]{2,1,0:T(8,128)(2,1)S(1)}, bf16[16,24,3072]{2,1,0:T(8,128)(2,1)}, u32[]{:S(2)}) copy-start(bf16[16,24,3072]{2,1,0:T(8,128)(2,1)} %param.8) | copy-start | bytes 7077892
  106.4 5.8 %collective-permute-start = (bf16[16,24,3072]{2,1,0:T(8,128)(2,1)}, bf16[16,24,3072]{2,1,0:T(8,128)(2,1)}, u32[]{:S(2)}, u32[]{:S(2)}) collective-permute-start(bf16[16,24,3072]{2,1,0:T(8,128)(2,1)} %dynamic-slice_bitcast_fusion), channel_id=1, source_target_pairs={{0,1},{1,0},{2,3},{3,2},{4,5},{5,4},{6,7},{7,6},{8,9},{9,8},{10,11... | collective-permute-start | bytes 7077896 | tf_op jit(solution)/shard_map/ppermute | solution.py:282
Sparse Core Ops, SparseCore 0:
  9.5 16.2 all-gather.3
  91.7 15.0 all-gather.5
where the time goes:
time: 182 us; the launch traced here: 181 us
  Pallas kernels  79.5 us (44%)
  local copies, waits for them, and re-layouts  24.4 us (13%)
  waiting for transfers between devices  23.1 us (13%)
  other arithmetic  21.8 us (12%)
  between operations  14.2 us (8%)
  matrix products  10.8 us (6%)
  starting transfers between devices  7.73 us (4%)
    pallas_call x1, Pallas kernels, attend(): pl.pallas_call(functools.partial(attend_kernel, 384), grid=(per_dev // GR...  46.6 us
    pallas_call x1, Pallas kernels, cache_rows(): pl.pallas_call(cache_kernel, grid=(per_dev // GROUP,), in_specs=[single(x...  28.6 us
    another operation x2, local copies, waits for them, and re-layouts, on_device(): jnp.stack([keys, values], 1).reshape(n_req * CAP, slot, 2, w_k.shape[1])  15.9 us
    all_gather x1, waiting for transfers between devices, on_device(): x_all = lax.all_gather(hidden_in, 'tp', axis=0, tiled=True)  15.7 us
    another operation x1, other arithmetic, on_device(): jnp.stack([keys, values], 1).reshape(n_req * CAP, slot, 2, w_k.shape[1])  12.8 us
    dot_general x1, matrix products, on_device(): jnp.dot(attn, w_o, preferred_element_type=jnp.float32).astype(jnp.bfloat16)  10.8 us
    all_to_all x1, starting transfers between devices, exchange(): return lax.all_to_all(blocks, axis, split_axis=0, concat_axis=0, tiled=True)  6.4 us
    convert_element_type x1, other arithmetic, on_device(): hidden_out = (total + hidden_in.astype(jnp.float32)).astype(jnp.bfloat16)  4.99 us
  transfers between devices with their start and end apart: 4, of which 3 were waited for; matrix products, arithmetic and copies ran while one was open for 13% of the time, Pallas kernels for 26%

commit v1 on v0

--- a/solution.py
+++ b/solution.py
@@ -142,7 +142,7 @@
     )(x, gain, w_q, w_k, w_v, *tables, bias)
 
 
-def cache_kernel(x_ref, gain_ref, wk_ref, wv_ref, cos_ref, low_ref, high_ref, k_ref, v_ref, normed_ref):
+def cache_kernel(x_ref, gain_ref, wk_ref, wv_ref, cos_ref, low_ref, high_ref, out_ref, normed_ref):
     cap, sources, slot, width = x_ref.shape
 
     @pl.when(pl.program_id(0) == 0)
@@ -164,8 +164,9 @@
         at = pl.ds(pl.multiple_of(i * chunk, chunk), chunk)
         n = normed_ref[at, :]
         dot = functools.partial(jnp.dot, preferred_element_type=jnp.float32)
-        k_ref[at, :] = rotate(dot(n, wk_ref[...]), cosine, low, high).astype(jnp.bfloat16)
-        v_ref[at, :] = dot(n, wv_ref[...]).astype(jnp.bfloat16)
+        keys = rotate(dot(n, wk_ref[...]), cosine, low, high)
+        values = dot(n, wv_ref[...])
+        out_ref[at] = jnp.stack([keys, values], 1).astype(jnp.bfloat16)
         return carry
 
     lax.fori_loop(0, rows // chunk, body, 0)
@@ -180,7 +181,7 @@
         shape, lambda g: (0,) * len(shape), pipeline_mode=pl.Buffered(1)
     )
     weight = pl.BlockSpec((width, GROUP), lambda g: (0, g))
-    out = pl.BlockSpec((rows, GROUP), lambda g: (0, g))
+    out = pl.BlockSpec((rows, 2, GROUP), lambda g: (0, 0, g))
     return pl.pallas_call(
         cache_kernel,
         grid=(per_dev // GROUP,),
@@ -188,8 +189,8 @@
             single(x.shape), whole((1, width)), weight, weight,
             whole((slot, GROUP)), whole((slot, GROUP)), whole((slot, GROUP)),
         ],
-        out_specs=[out, out],
-        out_shape=[jax.ShapeDtypeStruct((rows, per_dev), jnp.bfloat16)] * 2,
+        out_specs=out,
+        out_shape=jax.ShapeDtypeStruct((rows, 2, per_dev), jnp.bfloat16),
         scratch_shapes=[pltpu.VMEM((rows, width), jnp.bfloat16)],
         compiler_params=pltpu.CompilerParams(vmem_limit_bytes=VMEM),
         cost_estimate=pl.CostEstimate(
@@ -244,7 +245,12 @@
     gain = norm_gain[None, :]
     lens = lengths[0]
 
-    x_all = lax.all_gather(hidden_in, "tp", axis=0, tiled=True)
+    x_all = jnp.zeros((group, req_dev, slot, width), hidden_in.dtype)
+    x_all = lax.dynamic_update_index_in_dim(x_all, hidden_in, me, 0)
+    for step in range(1, group):
+        came = lax.ppermute(hidden_in, "tp", [(i, (i + step) % group) for i in range(group)])
+        x_all = lax.dynamic_update_index_in_dim(x_all, came, (me - step) % group, 0)
+    x_all = x_all.reshape(req_rep, slot, width)
 
     target = dest[0, :, 0]
     same = target[:, None] == target[None, :]
@@ -287,8 +293,8 @@
     if shares > 1:
         kept = kept.reshape(shares, CAP, n_req, slot, part)
         kept = kept.transpose(1, 2, 3, 0, 4).reshape(CAP, n_req, slot, width)
-    keys, values = cache_rows(kept, gain, w_k, w_v, tables)
-    cache = jnp.stack([keys, values], 1).reshape(n_req * CAP, slot, 2, w_k.shape[1])
+    cache = cache_rows(kept, gain, w_k, w_v, tables)
+    cache = cache.reshape(n_req * CAP, slot, 2, w_k.shape[1])
     return hidden_out, cache
 
 

time: 182 us -> 146 us (0.80)
  other arithmetic: 21.8 us -> 6.6 us
  local copies, waits for them, and re-layouts: 24.4 us -> 9.62 us
  waiting for transfers between devices: 23.1 us -> 9.34 us
  Pallas kernels: 79.5 us -> 86 us
    another operation x2 -> x0, local copies, waits for them, and re-layouts: 15.9 us -> none  [on_device(): jnp.stack([keys, values], 1).reshape(n_req * CAP, slot, 2, w_k.shape[1])]
    all_gather x1 -> x0, waiting for transfers between devices: 15.7 us -> none  [on_device(): x_all = lax.all_gather(hidden_in, 'tp', axis=0, tiled=True)]
    another operation x1 -> x0, other arithmetic: 12.8 us -> none  [on_device(): jnp.stack([keys, values], 1).reshape(n_req * CAP, slot, 2, w_k.shape[1])]
    pallas_call x1, Pallas kernels: 28.6 us -> 35 us  [cache_rows(): pl.pallas_call(cache_kernel, grid=(per_dev // GROUP,), in_specs=[single(x...]
    convert_element_type x1, other arithmetic: 4.99 us -> 2.66 us  [on_device(): hidden_out = (total + hidden_in.astype(jnp.float32)).astype(jnp.bfloat16)]
    dynamic_update_slice x0 -> x2, local copies, waits for them, and re-layouts: none -> 2.24 us  [the longest x1 1.95 us: on_device(): x_all = lax.dynamic_update_index_in_dim(x_all, came, (me - step) % group, 0)]
    unnamed x9 -> x11, local copies, waits for them, and re-layouts: 4.42 us -> 4.12 us
  transfers between devices with their start and end apart: 4 -> 4, of which waited for: 3 -> 3; matrix products, arithmetic and copies ran while one was open for 13% -> 15% of each run, Pallas kernels for 26% -> 32%
where the time goes in v1:
time: 146 us; the launch traced here: 145 us
  Pallas kernels  86 us (59%)
  between operations  14.2 us (10%)
  matrix products  10.8 us (7%)
  local copies, waits for them, and re-layouts  9.62 us (7%)
  waiting for transfers between devices  9.34 us (6%)
  starting transfers between devices  8.78 us (6%)
  other arithmetic  6.6 us (5%)
    pallas_call x1, Pallas kernels, attend(): pl.pallas_call(functools.partial(attend_kernel, 384), grid=(per_dev // GR...  46.7 us
    pallas_call x1, Pallas kernels, cache_rows(): pl.pallas_call(cache_kernel, grid=(per_dev // GROUP,), in_specs=[single(x...  35 us
    dot_general x1, matrix products, on_device(): jnp.dot(attn, w_o, preferred_element_type=jnp.float32).astype(jnp.bfloat16)  10.8 us
    all_to_all x1, starting transfers between devices, exchange(): return lax.all_to_all(blocks, axis, split_axis=0, concat_axis=0, tiled=True)  6.58 us
    ppermute x1, waiting for transfers between devices, on_device(): lax.ppermute(sent, 'tp', [(i, (i + step) % group) for i in range(group)])  5.92 us
    pallas_call x1, Pallas kernels, pick(): pl.pallas_call(pick_kernel, in_specs=[pl.BlockSpec(memory_space=pltpu.SME...  4.26 us
    unnamed x11, local copies, waits for them, and re-layouts  4.12 us
  transfers between devices with their start and end apart: 4, of which 3 were waited for; matrix products, arithmetic and copies ran while one was open for 15% of the time, Pallas kernels for 32%

profile of v1, /device:TPU:15, one launch (start us, length us, event | category | flops | bytes accessed | tf_op | source)
XLA Modules:
  0.0 145.3 jit_solution(16931841852736657023)
XLA Ops:
  7.2 0.7 collective-permute-start
  7.9 0.9 convert_reduce_fusion
  8.8 1.3 select_reduce_fusion
  10.1 0.6 broadcast_in_dim.55
  10.7 0.3 bitcast_dynamic-update-slice_fusion.1
  11.0 1.4 collective-permute-done
  12.4 1.9 %bitcast_dynamic-update-slice_fusion = bf16[2,16,24,3072]{3,2,1,0:T(8,128)(2,1)S(1)} fusion(bf16[2,16,24,3072]{3,2,1,0:T(8,128)(2,1)S(1)} %bitcast_dynamic-update-slice_fusion.1, s32[]{:T(128)S(6)} %select_n.58, bf16[16,24,3072]{2,1,0:T(8,128)(2,1)} %collective-permute-done), kind=kLoop, calls=%fused_computation.4 | loop fusion | bytes 4718596 | tf_op jit(solution)/shard_map/jit(dynamic_update_index_in_dim)/dynamic_update_slice | solution.py:252
  14.4 2.2 %copy-done = bf16[2,16,24,3072]{3,2,1,0:T(8,128)(2,1)} copy-done((bf16[2,16,24,3072]{3,2,1,0:T(8,128)(2,1)}, bf16[2,16,24,3072]{3,2,1,0:T(8,128)(2,1)S(1)}, u32[]{:S(2)}) %copy-start) | copy-done | bytes 4718616
  16.6 4.3 %pick.1 = bf16[16,24,3072]{2,1,0:T(8,128)(2,1)} custom-call(s32[16]{0:T(128)} %get-tuple-element.3.source_ref, s32[16]{0:T(128)} %get-tuple-element.2.lens_ref, bf16[32,24,3072]{2,1,0:T(8,128)(2,1)} %bitcast.19), custom_call_target="tpu_custom_call" | custom-call | tf_op jit(solution)/shard_map/pick/pallas_call | solution.py:220
  20.8 6.6 %all-to-all-start = ((bf16[16,24,3072]{2,1,0:T(8,128)(2,1)}), bf16[16,24,3072]{2,1,0:T(8,128)(2,1)S(1)}, u32[]{:S(2)}, u32[]{:S(2)}) async-start(bf16[16,24,3072]{2,1,0:T(8,128)(2,1)} %pick.1), calls=%async_computation | async-start | bytes 4718592 | tf_op jit(solution)/shard_map/all_to_all | solution.py:235
  27.5 0.5 broadcast.124
  28.0 0.7 reduce.3
  29.3 0.7 tile.13.cos_ref
  30.0 0.7 tile.30.low_ref
  30.7 0.7 tile.32.high_ref
  31.5 0.8 and_select_fusion.bias_ref
  32.3 46.7 %attend.1 = bf16[768,1536]{1,0:T(8,128)(2,1)} custom-call(bf16[768,3072]{1,0:T(8,128)(2,1)} %bitcast.20, f32[1,3072]{1,0:T(1,128)} %bitcast.27, bf16[3072,1536]{1,0:T(8,128)(2,1)} %wq_ref.1, bf16[3072,1536]{1,0:T(8,128)(2,1)} %wk_ref.3, bf16[3072,1536]{1,0:T(8,128)(2,1)} %wv_ref.3, f32[24,384]{1,0:T(8,128)} %tile.13.cos_ref, f32[24,384]{1,0:T(8,128)} %tile.30.low_ref, ...), custom_call_target="tpu_custom_call" | custom-call | flops 21743271936 | bytes 35389440 | tf_op jit(solution)/shard_map/attend/pallas_call | solution.py:124
  79.0 2.0 %all-to-all-done = bf16[16,24,3072]{2,1,0:T(8,128)(2,1)S(1)} async-done(((bf16[16,24,3072]{2,1,0:T(8,128)(2,1)}), bf16[16,24,3072]{2,1,0:T(8,128)(2,1)S(1)}, u32[]{:S(2)}, u32[]{:S(2)}) %all-to-all-start) | async-done | bytes 2359328 | tf_op jit(solution)/shard_map/all_to_all | solution.py:235
  81.0 1.4 copy-done.1
  82.4 10.8 %convolution_convert_fusion = bf16[768,3072]{1,0:T(8,128)(2,1)S(1)} fusion(bf16[768,1536]{1,0:T(8,128)(2,1)} %attend.1, bf16[1536,3072]{1,0:T(8,128)(2,1)} %param.13), kind=kOutput, calls=%fused_computation | convolution fusion | flops 7250116608 | bytes 16515072 | tf_op jit(solution)/shard_map/dot_general | solution.py:282
  93.4 1.4 collective-permute-start.1
  94.8 5.9 %collective-permute-done.1 = bf16[16,24,3072]{2,1,0:T(8,128)(2,1)S(1)} collective-permute-done((bf16[16,24,3072]{2,1,0:T(8,128)(2,1)S(1)}, bf16[16,24,3072]{2,1,0:T(8,128)(2,1)S(1)}, u32[]{:S(2)}, u32[]{:S(2)}) %collective-permute-start.1) | collective-permute-done | bytes 2359328 | tf_op jit(solution)/shard_map/ppermute | solution.py:288
  100.7 2.7 %fusion.1 = bf16[16,24,3072]{2,1,0:T(8,128)(2,1)} fusion(bf16[16,24,3072]{2,1,0:T(8,128)(2,1)S(1)} %copy-done.3, bf16[16,24,3072]{2,1,0:T(8,128)(2,1)S(1)} %collective-permute-done.1, bf16[2,16,24,3072]{3,2,1,0:T(8,128)(2,1)S(1)} %bitcast.22, s32[]{:T(128)S(6)} %select_n.56), kind=kLoop, calls=%fused_computation.3 | loop fusion | flops 7077888 | bytes 9437188 | tf_op jit(solution)/shard_map/convert_element_type | solution.py:290
  103.4 35.0 %cache_rows.1 = bf16[768,2,1536]{2,1,0:T(2,128)(2,1)} custom-call(bf16[2,16,24,3072]{3,2,1,0:T(8,128)(2,1)} %bitcast.26, f32[1,3072]{1,0:T(1,128)} %bitcast.28, bf16[3072,1536]{1,0:T(8,128)(2,1)} %wk_ref.3, bf16[3072,1536]{1,0:T(8,128)(2,1)} %wv_ref.3, f32[24,384]{1,0:T(8,128)} %tile.13.cos_ref, f32[24,384]{1,0:T(8,128)} %tile.30.low_ref, ...), custom_call_target="tpu_custom_call" | custom-call | flops 14495514624 | bytes 28311552 | tf_op jit(solution)/shard_map/cache_rows/pallas_call | solution.py:185
  (29 shorter events, 0.9 us)
Async XLA Ops:
  7.2 3.6 %copy-start.2 = (bf16[16,24,3072]{2,1,0:T(8,128)(2,1)S(1)}, bf16[16,24,3072]{2,1,0:T(8,128)(2,1)}, u32[]{:S(2)}) copy-start(bf16[16,24,3072]{2,1,0:T(8,128)(2,1)} %param.8) | copy-start | bytes 7077892
  7.2 5.2 %collective-permute-start = (bf16[16,24,3072]{2,1,0:T(8,128)(2,1)}, bf16[16,24,3072]{2,1,0:T(8,128)(2,1)}, u32[]{:S(2)}, u32[]{:S(2)}) collective-permute-start(bf16[16,24,3072]{2,1,0:T(8,128)(2,1)} %param.8), channel_id=1, source_target_pairs={{0,1},{1,0},{2,3},{3,2},{4,5},{5,4},{6,7},{7,6},{8,9},{9,8},{10,11... | collective-permute-start | bytes 7077896 | tf_op jit(solution)/shard_map/ppermute | solution.py:251
  14.4 2.2 %copy-start = (bf16[2,16,24,3072]{3,2,1,0:T(8,128)(2,1)}, bf16[2,16,24,3072]{3,2,1,0:T(8,128)(2,1)S(1)}, u32[]{:S(2)}) copy-start(bf16[2,16,24,3072]{3,2,1,0:T(8,128)(2,1)S(1)} %bitcast_dynamic-update-slice_fusion) | copy-start | bytes 14155780
  16.6 11.4 %copy-start.4 = (s32[1,32]{1,0:T(1,128)S(1)}, s32[1,32]{1,0:T(1,128)}, u32[]{:S(2)}) copy-start(s32[1,32]{1,0:T(1,128)} %param.14) | copy-start | bytes 388
  20.8 60.2 %all-to-all-start = ((bf16[16,24,3072]{2,1,0:T(8,128)(2,1)}), bf16[16,24,3072]{2,1,0:T(8,128)(2,1)S(1)}, u32[]{:S(2)}, u32[]{:S(2)}) async-start(bf16[16,24,3072]{2,1,0:T(8,128)(2,1)} %pick.1), calls=%async_computation | async-start | bytes 4718592 | tf_op jit(solution)/shard_map/all_to_all | solution.py:235
  27.4 76.0 %all-gather.3.cloned.1.call-start = ((), (), s32[]{:S(2)}) async-start(), calls=%async_computation.1 | async-start | bytes 7077888 | tf_op jit(solution)/shard_map/all_gather | solution.py:292
  81.0 1.4 copy-start.1
  93.2 7.5 %copy-start.3 = (bf16[16,24,3072]{2,1,0:T(8,128)(2,1)S(1)}, bf16[16,24,3072]{2,1,0:T(8,128)(2,1)}, u32[]{:S(2)}) copy-start(bf16[16,24,3072]{2,1,0:T(8,128)(2,1)} %param.8) | copy-start | bytes 7077892
  93.4 7.4 %collective-permute-start.1 = (bf16[16,24,3072]{2,1,0:T(8,128)(2,1)S(1)}, bf16[16,24,3072]{2,1,0:T(8,128)(2,1)S(1)}, u32[]{:S(2)}, u32[]{:S(2)}) collective-permute-start(bf16[16,24,3072]{2,1,0:T(8,128)(2,1)S(1)} %dynamic-slice_bitcast_fusion), channel_id=1, source_target_pairs={{0,1},{1,0},{2,3},{3,2},{4,5},{5,4},{6,7},{7,6},{8,9},{9,8},{10,11... | collective-permute-start | bytes 7077896 | tf_op jit(solution)/shard_map/ppermute | solution.py:288
Sparse Core Ops, SparseCore 0:
  82.6 16.8 all-gather.2

commit v2 on v1

--- a/solution.py
+++ b/solution.py
@@ -13,7 +13,7 @@
 GROUP = 384
 PAIR = 2 * HD
 BLOCK = 96
-VMEM = 56 * 1024 * 1024
+VMEM = 58 * 1024 * 1024
 
 
 def rope_tables(slot):
@@ -106,10 +106,12 @@
         v = dot(n, wv_ref[...]).astype(jnp.bfloat16)
         for b in range(chunk // BLOCK):
             at = slice(b * BLOCK, (b + 1) * BLOCK)
-            o = attention(q[at], k[at], v[at], bias_ref[i * (chunk // BLOCK) + b])
-            out_ref[pl.ds(pl.multiple_of(base + b * BLOCK, BLOCK), BLOCK), :] = o.astype(
-                jnp.bfloat16
-            )
+            to = pl.ds(pl.multiple_of(base + b * BLOCK, BLOCK), BLOCK)
+            seen = bias_ref[i * (chunk // BLOCK) + b]
+            for first in range(0, q.shape[1], GROUP):
+                heads = slice(first, first + GROUP)
+                o = attention(q[at, heads], k[at, heads], v[at, heads], seen)
+                out_ref[to, heads] = o.astype(jnp.bfloat16)
         return carry
 
     lax.fori_loop(0, rows // chunk, body, 0)
@@ -120,16 +122,19 @@
     per_dev = w_q.shape[1]
     slot = tables[0].shape[0]
     whole = lambda shape: pl.BlockSpec(shape, lambda g: (0,) * len(shape))
-    weight = pl.BlockSpec((width, GROUP), lambda g: (0, g))
+    cols = min(2 * GROUP, per_dev)
+    tables = [jnp.tile(t, (1, cols // GROUP)) for t in tables]
+    weight = pl.BlockSpec((width, cols), lambda g: (0, g))
     return pl.pallas_call(
         functools.partial(attend_kernel, 384),
-        grid=(per_dev // GROUP,),
+        grid=(per_dev // cols,),
         in_specs=[
-            whole((rows, width)), whole((1, width)), weight, weight, weight,
-            whole((slot, GROUP)), whole((slot, GROUP)), whole((slot, GROUP)),
+            pl.BlockSpec((rows, width), lambda g: (0, 0), pipeline_mode=pl.Buffered(1)),
+            whole((1, width)), weight, weight, weight,
+            whole((slot, cols)), whole((slot, cols)), whole((slot, cols)),
             whole(bias.shape),
         ],
-        out_specs=pl.BlockSpec((rows, GROUP), lambda g: (0, g)),
+        out_specs=pl.BlockSpec((rows, cols), lambda g: (0, g)),
         out_shape=jax.ShapeDtypeStruct((rows, per_dev), jnp.bfloat16),
         scratch_shapes=[pltpu.VMEM((rows, width), jnp.bfloat16)],
         compiler_params=pltpu.CompilerParams(vmem_limit_bytes=VMEM),
@@ -180,14 +185,16 @@
     single = lambda shape: pl.BlockSpec(
         shape, lambda g: (0,) * len(shape), pipeline_mode=pl.Buffered(1)
     )
-    weight = pl.BlockSpec((width, GROUP), lambda g: (0, g))
-    out = pl.BlockSpec((rows, 2, GROUP), lambda g: (0, 0, g))
+    cols = min(2 * GROUP, per_dev)
+    tables = [jnp.tile(t, (1, cols // GROUP)) for t in tables]
+    weight = pl.BlockSpec((width, cols), lambda g: (0, g))
+    out = pl.BlockSpec((rows, 2, cols), lambda g: (0, 0, g))
     return pl.pallas_call(
         cache_kernel,
-        grid=(per_dev // GROUP,),
+        grid=(per_dev // cols,),
         in_specs=[
             single(x.shape), whole((1, width)), weight, weight,
-            whole((slot, GROUP)), whole((slot, GROUP)), whole((slot, GROUP)),
+            whole((slot, cols)), whole((slot, cols)), whole((slot, cols)),
         ],
         out_specs=out,
         out_shape=jax.ShapeDtypeStruct((rows, 2, per_dev), jnp.bfloat16),

time: 146 us -> 146 us (level)
  waiting for transfers between devices: 9.34 us -> 5.99 us
  Pallas kernels: 86 us -> 89.3 us
    pallas_call x2, Pallas kernels: 81.8 us -> 85 us  [the longest x1 52.6 us: attend(): pl.pallas_call(functools.partial(attend_kernel, 384), grid=(per_dev // co...]
    all_to_all x1, waiting for transfers between devices: 2 us -> 0.01 us  [exchange(): return lax.all_to_all(blocks, axis, split_axis=0, concat_axis=0, tiled=True)]
    unnamed x11 -> x14, local copies, waits for them, and re-layouts: 4.12 us -> 6 us
    ppermute x1, waiting for transfers between devices: 5.92 us -> 4.16 us  [on_device(): lax.ppermute(sent, 'tp', [(i, (i + step) % group) for i in range(group)])]
  transfers between devices with their start and end apart: 4 -> 4, of which waited for: 3 -> 3; matrix products, arithmetic and copies ran while one was open for 15% -> 15% of each run, Pallas kernels for 32% -> 36%
where the time goes in v2:
time: 146 us; the launch traced here: 145 us
  Pallas kernels  89.3 us (61%)
  between operations  14.2 us (10%)
  matrix products  10.8 us (7%)
  local copies, waits for them, and re-layouts  9.75 us (7%)
  starting transfers between devices  8.36 us (6%)
  other arithmetic  6.69 us (5%)
  waiting for transfers between devices  5.99 us (4%)
    pallas_call x1, Pallas kernels, attend(): pl.pallas_call(functools.partial(attend_kernel, 384), grid=(per_dev // co...  52.6 us
    pallas_call x1, Pallas kernels, cache_rows(): pl.pallas_call(cache_kernel, grid=(per_dev // cols,), in_specs=[single(x....  32.4 us
    dot_general x1, matrix products, on_device(): jnp.dot(attn, w_o, preferred_element_type=jnp.float32).astype(jnp.bfloat16)  10.8 us
    all_to_all x1, starting transfers between devices, exchange(): return lax.all_to_all(blocks, axis, split_axis=0, concat_axis=0, tiled=True)  6.58 us
    unnamed x14, local copies, waits for them, and re-layouts  6 us
    pallas_call x1, Pallas kernels, pick(): pl.pallas_call(pick_kernel, in_specs=[pl.BlockSpec(memory_space=pltpu.SME...  4.26 us
    ppermute x1, waiting for transfers between devices, on_device(): lax.ppermute(sent, 'tp', [(i, (i + step) % group) for i in range(group)])  4.16 us
  transfers between devices with their start and end apart: 4, of which 3 were waited for; matrix products, arithmetic and copies ran while one was open for 15% of the time, Pallas kernels for 36%

profile of v2, /device:TPU:15, one launch (start us, length us, event | category | flops | bytes accessed | tf_op | source)
XLA Modules:
  0.0 145.0 jit_solution(4487075240710793159)
XLA Ops:
  7.2 0.7 collective-permute-start
  7.9 1.0 convert_reduce_fusion
  8.9 1.3 select_reduce_fusion
  10.2 0.6 broadcast_in_dim.55
  10.8 0.3 bitcast_dynamic-update-slice_fusion.1
  11.1 1.3 collective-permute-done
  12.4 1.9 %bitcast_dynamic-update-slice_fusion = bf16[2,16,24,3072]{3,2,1,0:T(8,128)(2,1)S(1)} fusion(bf16[2,16,24,3072]{3,2,1,0:T(8,128)(2,1)S(1)} %bitcast_dynamic-update-slice_fusion.1, s32[]{:T(128)S(6)} %select_n.58, bf16[16,24,3072]{2,1,0:T(8,128)(2,1)} %collective-permute-done), kind=kLoop, calls=%fused_computation.4 | loop fusion | bytes 4718596 | tf_op jit(solution)/shard_map/jit(dynamic_update_index_in_dim)/dynamic_update_slice | solution.py:259
  14.4 2.2 %copy-done = bf16[2,16,24,3072]{3,2,1,0:T(8,128)(2,1)} copy-done((bf16[2,16,24,3072]{3,2,1,0:T(8,128)(2,1)}, bf16[2,16,24,3072]{3,2,1,0:T(8,128)(2,1)S(1)}, u32[]{:S(2)}) %copy-start) | copy-done | bytes 4718616
  16.6 4.3 %pick.1 = bf16[16,24,3072]{2,1,0:T(8,128)(2,1)} custom-call(s32[16]{0:T(128)} %get-tuple-element.3.source_ref, s32[16]{0:T(128)} %get-tuple-element.2.lens_ref, bf16[32,24,3072]{2,1,0:T(8,128)(2,1)} %bitcast.25), custom_call_target="tpu_custom_call" | custom-call | tf_op jit(solution)/shard_map/pick/pallas_call | solution.py:227
  20.8 6.6 %all-to-all-start = ((bf16[16,24,3072]{2,1,0:T(8,128)(2,1)}), bf16[16,24,3072]{2,1,0:T(8,128)(2,1)S(1)}, u32[]{:S(2)}, u32[]{:S(2)}) async-start(bf16[16,24,3072]{2,1,0:T(8,128)(2,1)} %pick.1), calls=%async_computation | async-start | bytes 4718592 | tf_op jit(solution)/shard_map/all_to_all | solution.py:242
  27.5 0.5 broadcast.136
  28.0 0.7 reduce.3
  29.4 0.6 copy.10
  30.1 0.6 copy.11
  30.9 0.6 copy.12
  31.6 0.8 and_select_fusion.bias_ref
  32.4 52.6 %attend.1 = bf16[768,1536]{1,0:T(8,128)(2,1)} custom-call(bf16[768,3072]{1,0:T(8,128)(2,1)} %bitcast.26, f32[1,3072]{1,0:T(1,128)} %bitcast.42, bf16[3072,1536]{1,0:T(8,128)(2,1)} %wq_ref.1, bf16[3072,1536]{1,0:T(8,128)(2,1)} %wk_ref.3, bf16[3072,1536]{1,0:T(8,128)(2,1)} %wv_ref.3, f32[24,768]{1,0:T(8,128)} %bitcast.32, f32[24,768]{1,0:T(8,128)} %bitcast.34, ...), custom_call_target="tpu_custom_call" | custom-call | flops 21743271936 | bytes 35389440 | tf_op jit(solution)/shard_map/attend/pallas_call | solution.py:128
  85.1 1.4 copy-done.1
  86.5 10.8 %convolution_convert_fusion = bf16[768,3072]{1,0:T(8,128)(2,1)S(1)} fusion(bf16[768,1536]{1,0:T(8,128)(2,1)} %attend.1, bf16[1536,3072]{1,0:T(8,128)(2,1)} %param.13), kind=kOutput, calls=%fused_computation | convolution fusion | flops 7250116608 | bytes 16515072 | tf_op jit(solution)/shard_map/dot_general | solution.py:289
  97.4 1.0 collective-permute-start.1
  98.4 4.2 %collective-permute-done.1 = bf16[16,24,3072]{2,1,0:T(8,128)(2,1)S(1)} collective-permute-done((bf16[16,24,3072]{2,1,0:T(8,128)(2,1)S(1)}, bf16[16,24,3072]{2,1,0:T(8,128)(2,1)S(1)}, u32[]{:S(2)}, u32[]{:S(2)}) %collective-permute-start.1) | collective-permute-done | bytes 2359328 | tf_op jit(solution)/shard_map/ppermute | solution.py:295
  102.6 2.7 %fusion.1 = bf16[16,24,3072]{2,1,0:T(8,128)(2,1)} fusion(bf16[16,24,3072]{2,1,0:T(8,128)(2,1)S(1)} %copy-done.3, bf16[16,24,3072]{2,1,0:T(8,128)(2,1)S(1)} %collective-permute-done.1, bf16[2,16,24,3072]{3,2,1,0:T(8,128)(2,1)S(1)} %bitcast.28, s32[]{:T(128)S(6)} %select_n.56), kind=kLoop, calls=%fused_computation.3 | loop fusion | flops 7077888 | bytes 9437188 | tf_op jit(solution)/shard_map/convert_element_type | solution.py:297
  105.3 0.5 all-gather.3.cloned.1.call-done
  105.8 32.4 %cache_rows.1 = bf16[768,2,1536]{2,1,0:T(2,128)(2,1)} custom-call(bf16[2,16,24,3072]{3,2,1,0:T(8,128)(2,1)} %bitcast.41, f32[1,3072]{1,0:T(1,128)} %bitcast.43, bf16[3072,1536]{1,0:T(8,128)(2,1)} %wk_ref.3, bf16[3072,1536]{1,0:T(8,128)(2,1)} %wv_ref.3, f32[24,768]{1,0:T(8,128)} %bitcast.33, f32[24,768]{1,0:T(8,128)} %bitcast.35, f32[24,768]{1,0:T(8,128)} %bitcast.37), custom_call_target="tpu_custom_call" | custom-call | flops 14495514624 | bytes 28311552 | tf_op jit(solution)/shard_map/cache_rows/pallas_call | solution.py:192
  (35 shorter events, 1.3 us)
Async XLA Ops:
  7.2 5.2 %collective-permute-start = (bf16[16,24,3072]{2,1,0:T(8,128)(2,1)}, bf16[16,24,3072]{2,1,0:T(8,128)(2,1)}, u32[]{:S(2)}, u32[]{:S(2)}) collective-permute-start(bf16[16,24,3072]{2,1,0:T(8,128)(2,1)} %param.8), channel_id=1, source_target_pairs={{0,1},{1,0},{2,3},{3,2},{4,5},{5,4},{6,7},{7,6},{8,9},{9,8},{10,11... | collective-permute-start | bytes 7077896 | tf_op jit(solution)/shard_map/ppermute | solution.py:258
  7.9 2.9 %copy-start.2 = (bf16[16,24,3072]{2,1,0:T(8,128)(2,1)S(1)}, bf16[16,24,3072]{2,1,0:T(8,128)(2,1)}, u32[]{:S(2)}) copy-start(bf16[16,24,3072]{2,1,0:T(8,128)(2,1)} %param.8) | copy-start | bytes 7077892
  14.4 2.2 %copy-start = (bf16[2,16,24,3072]{3,2,1,0:T(8,128)(2,1)}, bf16[2,16,24,3072]{3,2,1,0:T(8,128)(2,1)S(1)}, u32[]{:S(2)}) copy-start(bf16[2,16,24,3072]{3,2,1,0:T(8,128)(2,1)S(1)} %bitcast_dynamic-update-slice_fusion) | copy-start | bytes 14155780
  16.6 11.4 %copy-start.4 = (s32[1,32]{1,0:T(1,128)S(1)}, s32[1,32]{1,0:T(1,128)}, u32[]{:S(2)}) copy-start(s32[1,32]{1,0:T(1,128)} %param.14) | copy-start | bytes 388
  20.8 64.2 %all-to-all-start = ((bf16[16,24,3072]{2,1,0:T(8,128)(2,1)}), bf16[16,24,3072]{2,1,0:T(8,128)(2,1)S(1)}, u32[]{:S(2)}, u32[]{:S(2)}) async-start(bf16[16,24,3072]{2,1,0:T(8,128)(2,1)} %pick.1), calls=%async_computation | async-start | bytes 4718592 | tf_op jit(solution)/shard_map/all_to_all | solution.py:242
  27.4 78.4 %all-gather.3.cloned.1.call-start = ((), (), s32[]{:S(2)}) async-start(), calls=%async_computation.1 | async-start | bytes 7077888 | tf_op jit(solution)/shard_map/all_gather | solution.py:299
  85.1 1.4 copy-start.1
  97.3 5.3 %copy-start.3 = (bf16[16,24,3072]{2,1,0:T(8,128)(2,1)S(1)}, bf16[16,24,3072]{2,1,0:T(8,128)(2,1)}, u32[]{:S(2)}) copy-start(bf16[16,24,3072]{2,1,0:T(8,128)(2,1)} %param.8) | copy-start | bytes 7077892
  97.4 5.2 %collective-permute-start.1 = (bf16[16,24,3072]{2,1,0:T(8,128)(2,1)S(1)}, bf16[16,24,3072]{2,1,0:T(8,128)(2,1)S(1)}, u32[]{:S(2)}, u32[]{:S(2)}) collective-permute-start(bf16[16,24,3072]{2,1,0:T(8,128)(2,1)S(1)} %dynamic-slice_bitcast_fusion), channel_id=1, source_target_pairs={{0,1},{1,0},{2,3},{3,2},{4,5},{5,4},{6,7},{7,6},{8,9},{9,8},{10,11... | collective-permute-start | bytes 7077896 | tf_op jit(solution)/shard_map/ppermute | solution.py:295
Sparse Core Ops, SparseCore 0:
  86.6 19.1 all-gather.2
